TPU v7x, 512 devices: a whole 4x4x16 slice. The times are simulated.
512 devices in a mesh: grp: 16 (over y, x), tile: 32 (over z, core).
Axes of the slice: x: 4, y: 4, z: 16, core: 2. Of those that a mesh axis runs over, the one named last changes fastest.
Arguments:
- latent: bfloat16 [8, 64, 64, 512], P(None, 'grp', 'tile'), may hold values from -36 to 36
- coarse_filters: bfloat16 [3, 3, 3, 512, 512], P(None, None, None, None, 'grp'), may hold values from -0.0546875 to 0.0546875
- mid_filters: bfloat16 [3, 3, 3, 256, 256], P(None, None, None, None, 'tile'), may hold values from -0.078125 to 0.078125
- fine_filters: bfloat16 [3, 3, 3, 128, 128], replicated, may hold values from -0.109375 to 0.109375
- coarse_proj: bfloat16 [512, 256], replicated, may hold values from -0.25 to 0.25
- mid_proj: bfloat16 [256, 128], replicated, may hold values from -0.375 to 0.375
Outputs:
- frames_out: bfloat16 [8, 256, 256, 128], P(None, 'grp', 'tile')
All inputs are finite; a program needn't handle non-finite values.
Results may differ from a plain program's by a relative error of at most 0.018.
Values may be sent and summed in bfloat16 or wider, within the bound.
A program may use at most 128 MiB of HBM per device.

v0:
```python
import jax
import jax.numpy as jnp
from jax import lax
from jax.sharding import PartitionSpec as P


def with_halo(shard, sides, width):
    for axis, dim in sides:
        size, length = (lax.axis_size(axis), shard.shape[dim])
        up = [(i, (i + 1) % size) for i in range(size - 1)]
        down = [(j, i) for i, j in up]
        last = lax.slice_in_dim(shard, length - width, length, axis=dim)
        initial = lax.slice_in_dim(shard, 0, width, axis=dim)
        before = lax.ppermute(last, axis, up)
        after = lax.ppermute(initial, axis, down)
        shard = jnp.concatenate([before, shard, after], axis=dim)
    return shard


def activate(values):
    widened = values.astype(jnp.float32)
    scaled = widened * lax.rsqrt(jnp.mean(widened * widened, axis=-1, keepdims=True) + 1e-06)
    return jax.nn.silu(scaled).astype(jnp.bfloat16)


def double_size(values):
    return jnp.repeat(jnp.repeat(values, 2, axis=1), 2, axis=2)


def time_padded(values):
    return jnp.pad(values, ((2, 0), (0, 0), (0, 0), (0, 0)))


def stencil_columns(extended):
    padded = time_padded(extended)
    height = extended.shape[1] - 2
    breadth = extended.shape[2] - 2
    return jnp.concatenate(
        [
            padded[:, row_step : row_step + height, col_step : col_step + breadth, :]
            for row_step in range(3)
            for col_step in range(3)
        ],
        axis=-1,
    )


def apply_columns(columns, filters):
    frames = columns.shape[0] - 2
    folded = filters.reshape(3, 9 * filters.shape[3], filters.shape[4])
    total = jnp.dot(columns[0:frames], folded[0], preferred_element_type=jnp.float32)
    for frame_step in (1, 2):
        total = total + jnp.dot(
            columns[frame_step : frame_step + frames],
            folded[frame_step],
            preferred_element_type=jnp.float32,
        )
    return total


def coarse_conv(extended, filters):
    padded = time_padded(extended)
    frames = extended.shape[0]
    height = extended.shape[1] - 2
    breadth = extended.shape[2] - 2
    inputs = filters.shape[3]
    outputs = filters.shape[4]
    total = jnp.zeros((frames, height, breadth, outputs), jnp.float32)
    for frame_step in range(3):
        spread = jnp.transpose(filters[frame_step], (2, 0, 1, 3)).reshape(inputs, 9 * outputs)
        products = jnp.dot(
            padded[frame_step : frame_step + frames], spread, preferred_element_type=jnp.float32
        )
        for row_step in range(3):
            for col_step in range(3):
                lane = 3 * row_step + col_step
                total = (
                    total
                    + products[
                        :,
                        row_step : row_step + height,
                        col_step : col_step + breadth,
                        lane * outputs : (lane + 1) * outputs,
                    ]
                )
    return total


def middle_conv(extended, mid_filters):
    columns = stencil_columns(extended)
    return apply_columns(columns, lax.all_gather(mid_filters, "tile", axis=4, tiled=True))


def body(latent, coarse_filters, mid_filters, fine_filters, coarse_proj, mid_proj):
    first_act = activate(latent)
    whole = lax.all_gather(first_act, "grp", axis=1, tiled=True)
    widened = with_halo(whole, (("tile", 2),), 1)
    padded = jnp.pad(widened, ((0, 0), (1, 1), (0, 0), (0, 0)))
    filtered = coarse_conv(padded, coarse_filters).astype(jnp.bfloat16)
    returned = lax.all_to_all(filtered, "grp", split_axis=1, concat_axis=3, tiled=True)
    level_zero = (latent.astype(jnp.float32) + returned.astype(jnp.float32)).astype(jnp.bfloat16)
    reduced = jnp.dot(level_zero, coarse_proj, preferred_element_type=jnp.float32).astype(
        jnp.bfloat16
    )
    mid_act = double_size(activate(reduced))
    mid_ext = with_halo(mid_act, (("grp", 1), ("tile", 2)), 1)
    mid_terms = middle_conv(mid_ext, mid_filters)
    mid_out = (double_size(reduced).astype(jnp.float32) + mid_terms).astype(jnp.bfloat16)
    fine_low = jnp.dot(mid_out, mid_proj, preferred_element_type=jnp.float32).astype(jnp.bfloat16)
    fine_in = double_size(fine_low)
    fine_act = double_size(activate(fine_low))
    fine_ext = with_halo(fine_act, (("grp", 1), ("tile", 2)), 1)
    fine_terms = apply_columns(stencil_columns(fine_ext), fine_filters)
    return (fine_in.astype(jnp.float32) + fine_terms).astype(jnp.bfloat16)


def solution(mesh):
    in_specs = (
        P(None, "grp", "tile", None),
        P(None, None, None, None, "grp"),
        P(None, None, None, None, "tile"),
        P(),
        P(),
        P(),
    )
    out_specs = P(None, "grp", "tile", None)
    return jax.shard_map(body, mesh=mesh, in_specs=in_specs, out_specs=out_specs, check_vma=False)
```

profile of v0, /device:TPU:7, one launch (start us, length us, event | category | flops | bytes accessed | tf_op | source)
XLA Modules:
  0.0 200.4 jit_solution(11646952750403236550)
XLA Ops:
  6.5 1.0 fusion.34
  7.6 1.6 fusion.33
  9.3 0.7 all-gather.5.cloned.1.call-update
  10.0 61.1 %all-gather.3.cloned.1.call-done = bf16[8,64,2,512]{3,0,2,1:T(8,128)(2,1)} async-done(((bf16[8,4,2,512]{3,0,2,1:T(8,128)(2,1)}), bf16[8,64,2,512]{3,0,2,1:T(8,128)(2,1)}) %all-gather.3.cloned.1.call-update) | async-done | bytes 1048592 | tf_op jit(solution)/shard_map/all_gather | solution.py:96
  71.1 1.8 copy.25
  73.0 5.1 %collective-permute-start = (bf16[8,64,1,512]{3,1,2,0:T(8,128)(2,1)S(1)}, bf16[8,64,1,512]{3,1,2,0:T(8,128)(2,1)S(1)}, u32[]{:S(2)}, u32[]{:S(2)}) collective-permute-start(bf16[8,64,1,512]{3,1,2,0:T(8,128)(2,1)S(1)} %get-tuple-element.8), channel_id=1, source_target_pairs={{0,1},{1,2},{2,3},{3,4},{4,5},{5,6},{6,7},{7,8},{8,9},{9,10},{10,1... | collective-permute-start | bytes 1572872 | tf_op jit(solution)/shard_map/ppermute | solution.py:14
  78.0 1.9 collective-permute-start.1
  80.0 4.1 %collective-permute-done = bf16[8,64,1,512]{3,1,2,0:T(8,128)(2,1)S(1)} collective-permute-done((bf16[8,64,1,512]{3,1,2,0:T(8,128)(2,1)S(1)}, bf16[8,64,1,512]{3,1,2,0:T(8,128)(2,1)S(1)}, u32[]{:S(2)}, u32[]{:S(2)}) %collective-permute-start) | collective-permute-done | bytes 524320 | tf_op jit(solution)/shard_map/ppermute | solution.py:14
  84.1 4.4 %collective-permute-done.1 = bf16[8,64,1,512]{3,1,2,0:T(8,128)(2,1)S(1)} collective-permute-done((bf16[8,64,1,512]{3,1,2,0:T(8,128)(2,1)S(1)}, bf16[8,64,1,512]{3,1,2,0:T(8,128)(2,1)S(1)}, u32[]{:S(2)}, u32[]{:S(2)}) %collective-permute-start.1) | collective-permute-done | bytes 524320 | tf_op jit(solution)/shard_map/ppermute | solution.py:15
  88.5 1.0 fusion.5
  89.6 1.4 fusion.47
  91.0 1.4 fusion.50
  92.5 1.4 fusion.51
  93.9 2.5 %fusion.24 = bf16[8,64,2,32]{3,1,2,0:T(8,128)(2,1)S(1)} fusion(f32[8,66,4,288]{3,1,2,0:T(8,128)S(1)} %fusion.47, f32[8,66,4,288]{3,1,2,0:T(8,128)S(1)} %fusion.51, f32[8,66,4,288]{3,1,2,0:T(8,128)S(1)} %fusion.50), kind=kLoop, calls=%fused_computation.35 | loop fusion | flops 884736 | bytes 3604480 | tf_op jit(solution)/shard_map/convert_element_type | solution.py:99
  97.0 9.8 %all_to_all.4 = bf16[16,2,1024]{2,1,0:T(2,128)(2,1)S(1)} all-to-all(bf16[16,2,1024]{2,1,0:T(2,128)(2,1)S(1)} %reshape.91), channel_id=1, replica_groups=mesh['grp'=16,'tile'=32] {'grp'}, dimensions={0} | all-to-all | bytes 131072 | tf_op jit(solution)/shard_map/all_to_all | solution.py:100
  108.0 3.7 %collective-permute-start.2 = (bf16[8,1,4,256]{3,2,1,0:T(4,128)(2,1)S(1)}, bf16[8,1,4,256]{3,2,1,0:T(4,128)(2,1)S(1)}, u32[]{:S(2)}, u32[]{:S(2)}) collective-permute-start(bf16[8,1,4,256]{3,2,1,0:T(4,128)(2,1)S(1)} %get-tuple-element.23), channel_id=1, source_target_pairs={{0,32},{32,64},{64,96},{96,128},{128,160},{160,192},{192,224},{224... | collective-permute-start | bytes 49160 | tf_op jit(solution)/shard_map/ppermute | solution.py:14
  111.7 1.9 collective-permute-start.3
  113.7 4.6 %collective-permute-done.3 = bf16[8,1,4,256]{3,2,1,0:T(4,128)(2,1)S(1)} collective-permute-done((bf16[8,1,4,256]{3,2,1,0:T(4,128)(2,1)S(1)}, bf16[8,1,4,256]{3,2,1,0:T(4,128)(2,1)S(1)}, u32[]{:S(2)}, u32[]{:S(2)}) %collective-permute-start.3) | collective-permute-done | bytes 16416 | tf_op jit(solution)/shard_map/ppermute | solution.py:15
  118.4 4.6 %collective-permute-start.4 = (bf16[8,10,1,256]{3,2,1,0:T(2,128)(2,1)S(1)}, bf16[8,10,1,256]{3,2,1,0:T(2,128)(2,1)S(1)}, u32[]{:S(2)}, u32[]{:S(2)}) collective-permute-start(bf16[8,10,1,256]{3,2,1,0:T(2,128)(2,1)S(1)} %get-tuple-element.20), channel_id=1, source_target_pairs={{0,1},{1,2},{2,3},{3,4},{4,5},{5,6},{6,7},{7,8},{8,9},{9,10},{10,1... | collective-permute-start | bytes 122888 | tf_op jit(solution)/shard_map/ppermute | solution.py:14
  123.1 2.1 %collective-permute-start.5 = (bf16[8,10,1,256]{3,2,1,0:T(2,128)(2,1)S(1)}, bf16[8,10,1,256]{3,2,1,0:T(2,128)(2,1)S(1)}, u32[]{:S(2)}, u32[]{:S(2)}) collective-permute-start(bf16[8,10,1,256]{3,2,1,0:T(2,128)(2,1)S(1)} %get-tuple-element.21), channel_id=1, source_target_pairs={{1,0},{2,1},{3,2},{4,3},{5,4},{6,5},{7,6},{8,7},{9,8},{10,9},{11,1... | collective-permute-start | bytes 122888 | tf_op jit(solution)/shard_map/ppermute | solution.py:15
  125.6 3.7 %collective-permute-done.5 = bf16[8,10,1,256]{3,2,1,0:T(2,128)(2,1)S(1)} collective-permute-done((bf16[8,10,1,256]{3,2,1,0:T(2,128)(2,1)S(1)}, bf16[8,10,1,256]{3,2,1,0:T(2,128)(2,1)S(1)}, u32[]{:S(2)}, u32[]{:S(2)}) %collective-permute-start.5) | collective-permute-done | bytes 40992 | tf_op jit(solution)/shard_map/ppermute | solution.py:15
  129.6 0.7 slice_dynamic-update-slice_fusion.17
  130.4 0.8 slice_dynamic-update-slice_fusion.16
  131.2 0.8 slice_dynamic-update-slice_fusion.15
  132.0 0.8 slice_dynamic-update-slice_fusion.14
  132.8 0.8 slice_dynamic-update-slice_fusion.13
  133.6 0.8 slice_dynamic-update-slice_fusion.12
  134.4 0.8 slice_dynamic-update-slice_fusion.11
  135.2 0.8 slice_dynamic-update-slice_fusion.10
  136.0 0.8 slice_dynamic-update-slice_fusion.9
  136.8 16.2 %all-gather.5.cloned.1.call-done = bf16[3,3,3,256,256]{3,4,2,1,0:T(8,128)(2,1)} async-done(((bf16[3,3,3,256,8]{3,4,2,1,0:T(8,128)(2,1)}), bf16[3,3,3,256,256]{3,4,2,1,0:T(8,128)(2,1)}) %all-gather.5.cloned.1.call-update) | async-done | bytes 3538960 | tf_op jit(solution)/shard_map/all_gather | solution.py:91
  153.0 3.3 %fusion.40 = (bf16[1,3,3,256,256]{3,4,2,1,0:T(8,128)(2,1)S(1)}, bf16[1,3,3,256,256]{3,4,2,1,0:T(8,128)(2,1)S(1)}, bf16[1,3,3,256,256]{3,4,2,1,0:T(8,128)(2,1)}) fusion(bf16[3,3,3,256,256]{3,4,2,1,0:T(8,128)(2,1)} %all-gather.5.cloned.1.call-done), kind=kLoop, calls=%fused_computation.110 | loop fusion | bytes 7077888 | tf_op jit(solution)/shard_map/slice | solution.py:55
  156.3 2.4 %copy.49 = bf16[1,3,3,256,256]{4,3,2,1,0:T(8,128)(2,1)} copy(bf16[1,3,3,256,256]{3,4,2,1,0:T(8,128)(2,1)} %get-tuple-element.7) | data formatting | bytes 2359296
  158.7 1.6 copy.50
  160.2 0.7 copy.51
  161.0 2.4 %fusion.48 = f32[8,8,4,256]{3,2,1,0:T(4,128)S(1)} fusion(bf16[10,8,4,2304]{3,2,1,0:T(4,128)(2,1)} %slice_dynamic-update-slice_fusion.9, bf16[2304,256,1,1]{1,0,3,2:T(8,128)(2,1)} %bitcast.115), kind=kOutput, calls=%fused_computation.119 | convolution fusion | flops 301989888 | bytes 2916352 | tf_op jit(solution)/shard_map/dot_general | solution.py:51
  163.4 2.0 convolution_add_fusion.3
  165.4 2.1 %fusion.14 = bf16[8,8,4,256]{3,2,1,0:T(4,128)(2,1)S(1)} fusion(f32[8,8,4,256]{3,2,1,0:T(4,128)S(1)} %convert_element_type.86, f32[8,8,4,256]{3,2,1,0:T(4,128)S(1)} %convolution_add_fusion.3, bf16[10,8,4,2304]{3,2,1,0:T(4,128)(2,1)} %slice_dynamic-update-slice_fusion.9, bf16[2304,256,1,1]{1,0,3,2:T(8,128)(2,1)S(1)} %bitcast.114), kind=kOutput, calls=%fused_computation.21 | convolution fusion | flops 302186496 | bytes 3309568 | tf_op jit(solution)/shard_map/dot_general | solution.py:53
  168.2 2.7 %collective-permute-start.6 = (bf16[8,1,8,128]{3,2,1,0:T(8,128)(2,1)S(1)}, bf16[8,1,8,128]{3,2,1,0:T(8,128)(2,1)S(1)}, u32[]{:S(2)}, u32[]{:S(2)}) collective-permute-start(bf16[8,1,8,128]{3,2,1,0:T(8,128)(2,1)S(1)} %get-tuple-element.18), channel_id=1, source_target_pairs={{0,32},{32,64},{64,96},{96,128},{128,160},{160,192},{192,224},{224... | collective-permute-start | bytes 49160 | tf_op jit(solution)/shard_map/ppermute | solution.py:14
  170.9 2.6 %collective-permute-start.7 = (bf16[8,1,8,128]{3,2,1,0:T(8,128)(2,1)S(1)}, bf16[8,1,8,128]{3,2,1,0:T(8,128)(2,1)S(1)}, u32[]{:S(2)}, u32[]{:S(2)}) collective-permute-start(bf16[8,1,8,128]{3,2,1,0:T(8,128)(2,1)S(1)} %get-tuple-element.19), channel_id=1, source_target_pairs={{32,0},{64,32},{96,64},{128,96},{160,128},{192,160},{224,192},{256... | collective-permute-start | bytes 49160 | tf_op jit(solution)/shard_map/ppermute | solution.py:15
  173.5 4.0 %collective-permute-done.7 = bf16[8,1,8,128]{3,2,1,0:T(8,128)(2,1)S(1)} collective-permute-done((bf16[8,1,8,128]{3,2,1,0:T(8,128)(2,1)S(1)}, bf16[8,1,8,128]{3,2,1,0:T(8,128)(2,1)S(1)}, u32[]{:S(2)}, u32[]{:S(2)}) %collective-permute-start.7) | collective-permute-done | bytes 16416 | tf_op jit(solution)/shard_map/ppermute | solution.py:15
  177.6 5.2 %collective-permute-start.8 = (bf16[8,18,1,128]{3,2,1,0:T(2,128)(2,1)S(1)}, bf16[8,18,1,128]{3,2,1,0:T(2,128)(2,1)S(1)}, u32[]{:S(2)}, u32[]{:S(2)}) collective-permute-start(bf16[8,18,1,128]{3,2,1,0:T(2,128)(2,1)S(1)} %get-tuple-element.16), channel_id=1, source_target_pairs={{0,1},{1,2},{2,3},{3,4},{4,5},{5,6},{6,7},{7,8},{8,9},{9,10},{10,1... | collective-permute-start | bytes 110600 | tf_op jit(solution)/shard_map/ppermute | solution.py:14
  182.9 1.9 collective-permute-start.9
  184.9 3.6 %collective-permute-done.9 = bf16[8,18,1,128]{3,2,1,0:T(2,128)(2,1)S(1)} collective-permute-done((bf16[8,18,1,128]{3,2,1,0:T(2,128)(2,1)S(1)}, bf16[8,18,1,128]{3,2,1,0:T(2,128)(2,1)S(1)}, u32[]{:S(2)}, u32[]{:S(2)}) %collective-permute-start.9) | collective-permute-done | bytes 36896 | tf_op jit(solution)/shard_map/ppermute | solution.py:15
  188.5 0.4 fusion.21
  190.2 0.8 fusion.49
  191.0 0.8 convolution_add_fusion.1
  192.0 1.5 fusion.12
  (65 shorter events, 5.2 us)
Async XLA Ops:
  6.5 100.8 %copy-start = (bf16[512,256]{1,0:T(8,128)(2,1)S(1)}, bf16[512,256]{1,0:T(8,128)(2,1)}, u32[]{:S(2)}) copy-start(bf16[512,256]{1,0:T(8,128)(2,1)} %param.10) | copy-start | bytes 786436
  6.5 73.4 %copy-start.2 = (bf16[3,3,3,512,32]{3,4,2,1,0:T(8,128)(2,1)S(1)}, bf16[3,3,3,512,32]{3,4,2,1,0:T(8,128)(2,1)}, u32[]{:S(2)}) copy-start(bf16[3,3,3,512,32]{3,4,2,1,0:T(8,128)(2,1)} %param.7) | copy-start | bytes 2654212
  6.5 64.5 %all-gather.3.cloned.1.call-start = ((), (), s32[]{:S(2)}) async-start(), calls=%async_computation.1 | async-start | bytes 1114112 | tf_op jit(solution)/shard_map/all_gather | solution.py:96
  9.2 143.8 %all-gather.5.cloned.1.call-start = ((), (), s32[]{:S(2)}) async-start(), calls=%async_computation.2 | async-start | bytes 3649536 | tf_op jit(solution)/shard_map/all_gather | solution.py:91
  73.0 11.2 %collective-permute-start = (bf16[8,64,1,512]{3,1,2,0:T(8,128)(2,1)S(1)}, bf16[8,64,1,512]{3,1,2,0:T(8,128)(2,1)S(1)}, u32[]{:S(2)}, u32[]{:S(2)}) collective-permute-start(bf16[8,64,1,512]{3,1,2,0:T(8,128)(2,1)S(1)} %get-tuple-element.8), channel_id=1, source_target_pairs={{0,1},{1,2},{2,3},{3,4},{4,5},{5,6},{6,7},{7,8},{8,9},{9,10},{10,1... | collective-permute-start | bytes 1572872 | tf_op jit(solution)/shard_map/ppermute | solution.py:14
  78.0 10.5 %collective-permute-start.1 = (bf16[8,64,1,512]{3,1,2,0:T(8,128)(2,1)S(1)}, bf16[8,64,1,512]{3,1,2,0:T(8,128)(2,1)S(1)}, u32[]{:S(2)}, u32[]{:S(2)}) collective-permute-start(bf16[8,64,1,512]{3,1,2,0:T(8,128)(2,1)S(1)} %get-tuple-element.9), channel_id=1, source_target_pairs={{1,0},{2,1},{3,2},{4,3},{5,4},{6,5},{7,6},{8,7},{9,8},{10,9},{11,1... | collective-permute-start | bytes 1572872 | tf_op jit(solution)/shard_map/ppermute | solution.py:15
  96.4 10.9 %copy-start.4 = (bf16[8,4,2,512]{3,2,1,0:T(2,128)(2,1)S(1)}, bf16[8,4,2,512]{3,2,1,0:T(2,128)(2,1)}, u32[]{:S(2)}) copy-start(bf16[8,4,2,512]{3,2,1,0:T(2,128)(2,1)} %param.6) | copy-start | bytes 196612
  108.0 5.6 %collective-permute-start.2 = (bf16[8,1,4,256]{3,2,1,0:T(4,128)(2,1)S(1)}, bf16[8,1,4,256]{3,2,1,0:T(4,128)(2,1)S(1)}, u32[]{:S(2)}, u32[]{:S(2)}) collective-permute-start(bf16[8,1,4,256]{3,2,1,0:T(4,128)(2,1)S(1)} %get-tuple-element.23), channel_id=1, source_target_pairs={{0,32},{32,64},{64,96},{96,128},{128,160},{160,192},{192,224},{224... | collective-permute-start | bytes 49160 | tf_op jit(solution)/shard_map/ppermute | solution.py:14
  111.7 6.6 %collective-permute-start.3 = (bf16[8,1,4,256]{3,2,1,0:T(4,128)(2,1)S(1)}, bf16[8,1,4,256]{3,2,1,0:T(4,128)(2,1)S(1)}, u32[]{:S(2)}, u32[]{:S(2)}) collective-permute-start(bf16[8,1,4,256]{3,2,1,0:T(4,128)(2,1)S(1)} %get-tuple-element.22), channel_id=1, source_target_pairs={{32,0},{64,32},{96,64},{128,96},{160,128},{192,160},{224,192},{256... | collective-permute-start | bytes 49160 | tf_op jit(solution)/shard_map/ppermute | solution.py:15
  118.4 7.2 %collective-permute-start.4 = (bf16[8,10,1,256]{3,2,1,0:T(2,128)(2,1)S(1)}, bf16[8,10,1,256]{3,2,1,0:T(2,128)(2,1)S(1)}, u32[]{:S(2)}, u32[]{:S(2)}) collective-permute-start(bf16[8,10,1,256]{3,2,1,0:T(2,128)(2,1)S(1)} %get-tuple-element.20), channel_id=1, source_target_pairs={{0,1},{1,2},{2,3},{3,4},{4,5},{5,6},{6,7},{7,8},{8,9},{9,10},{10,1... | collective-permute-start | bytes 122888 | tf_op jit(solution)/shard_map/ppermute | solution.py:14
  123.1 6.3 %collective-permute-start.5 = (bf16[8,10,1,256]{3,2,1,0:T(2,128)(2,1)S(1)}, bf16[8,10,1,256]{3,2,1,0:T(2,128)(2,1)S(1)}, u32[]{:S(2)}, u32[]{:S(2)}) collective-permute-start(bf16[8,10,1,256]{3,2,1,0:T(2,128)(2,1)S(1)} %get-tuple-element.21), channel_id=1, source_target_pairs={{1,0},{2,1},{3,2},{4,3},{5,4},{6,5},{7,6},{8,7},{9,8},{10,9},{11,1... | collective-permute-start | bytes 122888 | tf_op jit(solution)/shard_map/ppermute | solution.py:15
  161.0 2.4 %copy-start.1 = (bf16[1,3,3,256,256]{4,3,2,1,0:T(8,128)(2,1)S(1)}, bf16[1,3,3,256,256]{4,3,2,1,0:T(8,128)(2,1)}, u32[]{:S(2)}) copy-start(bf16[1,3,3,256,256]{4,3,2,1,0:T(8,128)(2,1)} %copy.50) | copy-start | bytes 3538948
  165.4 2.1 %copy-start.5 = (bf16[256,128]{1,0:T(8,128)(2,1)S(1)}, bf16[256,128]{1,0:T(8,128)(2,1)}, u32[]{:S(2)}) copy-start(bf16[256,128]{1,0:T(8,128)(2,1)} %param.11) | copy-start | bytes 196612
  165.4 19.4 %copy-start.3 = (bf16[3,3,3,128,128]{4,3,2,1,0:T(8,128)(2,1)S(1)}, bf16[3,3,3,128,128]{4,3,2,1,0:T(8,128)(2,1)}, u32[]{:S(2)}) copy-start(bf16[3,3,3,128,128]{4,3,2,1,0:T(8,128)(2,1)} %param.9) | copy-start | bytes 2654212
  168.2 5.3 %collective-permute-start.6 = (bf16[8,1,8,128]{3,2,1,0:T(8,128)(2,1)S(1)}, bf16[8,1,8,128]{3,2,1,0:T(8,128)(2,1)S(1)}, u32[]{:S(2)}, u32[]{:S(2)}) collective-permute-start(bf16[8,1,8,128]{3,2,1,0:T(8,128)(2,1)S(1)} %get-tuple-element.18), channel_id=1, source_target_pairs={{0,32},{32,64},{64,96},{96,128},{128,160},{160,192},{192,224},{224... | collective-permute-start | bytes 49160 | tf_op jit(solution)/shard_map/ppermute | solution.py:14
  170.9 6.6 %collective-permute-start.7 = (bf16[8,1,8,128]{3,2,1,0:T(8,128)(2,1)S(1)}, bf16[8,1,8,128]{3,2,1,0:T(8,128)(2,1)S(1)}, u32[]{:S(2)}, u32[]{:S(2)}) collective-permute-start(bf16[8,1,8,128]{3,2,1,0:T(8,128)(2,1)S(1)} %get-tuple-element.19), channel_id=1, source_target_pairs={{32,0},{64,32},{96,64},{128,96},{160,128},{192,160},{224,192},{256... | collective-permute-start | bytes 49160 | tf_op jit(solution)/shard_map/ppermute | solution.py:15
  177.6 7.3 %collective-permute-start.8 = (bf16[8,18,1,128]{3,2,1,0:T(2,128)(2,1)S(1)}, bf16[8,18,1,128]{3,2,1,0:T(2,128)(2,1)S(1)}, u32[]{:S(2)}, u32[]{:S(2)}) collective-permute-start(bf16[8,18,1,128]{3,2,1,0:T(2,128)(2,1)S(1)} %get-tuple-element.16), channel_id=1, source_target_pairs={{0,1},{1,2},{2,3},{3,4},{4,5},{5,6},{6,7},{7,8},{8,9},{9,10},{10,1... | collective-permute-start | bytes 110600 | tf_op jit(solution)/shard_map/ppermute | solution.py:14
  182.9 5.7 %collective-permute-start.9 = (bf16[8,18,1,128]{3,2,1,0:T(2,128)(2,1)S(1)}, bf16[8,18,1,128]{3,2,1,0:T(2,128)(2,1)S(1)}, u32[]{:S(2)}, u32[]{:S(2)}) collective-permute-start(bf16[8,18,1,128]{3,2,1,0:T(2,128)(2,1)S(1)} %get-tuple-element.17), channel_id=1, source_target_pairs={{1,0},{2,1},{3,2},{4,3},{5,4},{6,5},{7,6},{8,7},{9,8},{10,9},{11,1... | collective-permute-start | bytes 110600 | tf_op jit(solution)/shard_map/ppermute | solution.py:15
Sparse Core Ops, SparseCore 0:
  10.4 60.6 all-gather.2
  73.1 79.7 all-gather.4
where the time goes:
time: 201 us; the launch traced here: 200 us
  waiting for transfers between devices  102 us (51%)
  starting transfers between devices  31.8 us (16%)
  local copies, waits for them, and re-layouts  20.9 us (10%)
  matrix products  14.4 us (7%)
  between operations  13.9 us (7%)
  blocking collectives  9.77 us (5%)
  other arithmetic  7.18 us (4%)
    all_gather x1, waiting for transfers between devices, body(): whole = lax.all_gather(first_act, 'grp', axis=1, tiled=True)  61.1 us
    ppermute x5, starting transfers between devices, with_halo(): before = lax.ppermute(last, axis, up)  21.3 us
    ppermute x5, waiting for transfers between devices, with_halo(): after = lax.ppermute(initial, axis, down)  20.3 us
    all_gather x1, waiting for transfers between devices, middle_conv(): lax.all_gather(mid_filters, 'tile', axis=4, tiled=True)  16.2 us
    unnamed x35, local copies, waits for them, and re-layouts  12.7 us
    ppermute x5, starting transfers between devices, with_halo(): after = lax.ppermute(initial, axis, down)  10.5 us
    all_to_all x1, blocking collectives, body(): lax.all_to_all(filtered, 'grp', split_axis=1, concat_axis=3, tiled=True)  9.77 us
    dot_general x4, matrix products, apply_columns(): jnp.dot(columns[frame_step:frame_step + frames], folded[frame_step], pref...  6.33 us
  transfers between devices with their start and end apart: 12, of which 8 were waited for; matrix products, arithmetic and copies ran while one was open for 10% of the time, Pallas kernels for 0%

commit v1 on v0

--- a/solution.py
+++ b/solution.py
@@ -1,7 +1,35 @@
+import functools
 import jax
 import jax.numpy as jnp
 from jax import lax
 from jax.sharding import PartitionSpec as P
+
+
+def _begin_stages_all(q_in, k_dim, content):
+    y1, m_next = (q_in.shape[:k_dim], q_in.shape[k_dim + 1 :])
+    return jnp.moveaxis(q_in.reshape(*y1, content, -1, *m_next), k_dim, 0)
+
+
+def assign_task(arr_in, in_dim):
+    arr_in = jnp.moveaxis(arr_in, 0, in_dim)
+    part_next = arr_in.shape
+    return arr_in.reshape(
+        *part_next[:in_dim], part_next[in_dim] * part_next[in_dim + 1], *part_next[in_dim + 2 :]
+    )
+
+
+def pack_column_here(packet, mesh_ax, w_in, field):
+    now, value_now = (jax.lax.axis_size(mesh_ax), jax.lax.axis_index(mesh_ax))
+    local_next = _begin_stages_all(packet, w_in, now)
+    gallery = [local_next[value_now]]
+    for idx in [*range(1, now)]:
+        state_next = local_next[value_now ^ idx]
+        gallery.append(jax.lax.ppermute(state_next, mesh_ax, [(i0, i0 ^ idx) for i0 in range(now)]))
+    local_next = jnp.stack(gallery, 0)[value_now ^ jnp.arange(now)]
+    return assign_task(local_next, field)
+
+
+shape_values = functools.partial(pack_column_here, mesh_ax="grp", w_in=1, field=3)
 
 
 def with_halo(shard, sides, width):
@@ -97,7 +125,7 @@
     widened = with_halo(whole, (("tile", 2),), 1)
     padded = jnp.pad(widened, ((0, 0), (1, 1), (0, 0), (0, 0)))
     filtered = coarse_conv(padded, coarse_filters).astype(jnp.bfloat16)
-    returned = lax.all_to_all(filtered, "grp", split_axis=1, concat_axis=3, tiled=True)
+    returned = shape_values(filtered)
     level_zero = (latent.astype(jnp.float32) + returned.astype(jnp.float32)).astype(jnp.bfloat16)
     reduced = jnp.dot(level_zero, coarse_proj, preferred_element_type=jnp.float32).astype(
         jnp.bfloat16

time: 201 us -> 240 us (1.19)
  the two profiles are of different devices: /device:TPU:7 before, /device:TPU:152 now
where the time goes in v1:
time: 240 us; the launch traced here: 239 us
  waiting for transfers between devices  90.4 us (38%)
  starting transfers between devices  89.3 us (37%)
  local copies, waits for them, and re-layouts  22.2 us (9%)
  between operations  15.9 us (7%)
  matrix products  14.4 us (6%)
  other arithmetic  7.2 us (3%)
    all_gather x1, waiting for transfers between devices, body(): whole = lax.all_gather(first_act, 'grp', axis=1, tiled=True)  61.4 us
    ppermute x15, starting transfers between devices, pack_column_here(): jax.lax.ppermute(state_next, mesh_ax, [(i0, i0 ^ idx) for i0 in range(now)])  59.9 us
    ppermute x5, waiting for transfers between devices, with_halo(): before = lax.ppermute(last, axis, up)  19 us
    ppermute x5, starting transfers between devices, with_halo(): after = lax.ppermute(initial, axis, down)  18.1 us
    unnamed x48, local copies, waits for them, and re-layouts  12.2 us
    ppermute x5, starting transfers between devices, with_halo(): before = lax.ppermute(last, axis, up)  11.2 us
    dot_general x4, matrix products, apply_columns(): jnp.dot(columns[frame_step:frame_step + frames], folded[frame_step], pref...  6.32 us
    ppermute x5, waiting for transfers between devices, with_halo(): after = lax.ppermute(initial, axis, down)  5.71 us
  transfers between devices with their start and end apart: 27, of which 8 were waited for; matrix products, arithmetic and copies ran while one was open for 8% of the time, Pallas kernels for 0%

profile of v1, /device:TPU:152, one launch (start us, length us, event | category | flops | bytes accessed | tf_op | source)
XLA Modules:
  0.0 239.4 jit_solution(16670165172685220320)
XLA Ops:
  7.4 1.0 fusion.34
  8.4 1.6 fusion.33
  10.1 61.4 %all-gather.3.cloned.1.call-done = bf16[8,64,2,512]{3,0,2,1:T(8,128)(2,1)} async-done(((bf16[8,4,2,512]{3,0,2,1:T(8,128)(2,1)}), bf16[8,64,2,512]{3,0,2,1:T(8,128)(2,1)}) %all-gather.3.cloned.1.call-update) | async-done | bytes 1048592 | tf_op jit(solution)/shard_map/all_gather | solution.py:124
  71.5 1.8 copy.68
  73.3 1.1 fusion.42
  74.4 1.9 collective-permute-start.1
  76.3 2.4 %collective-permute-start = (bf16[8,64,1,512]{3,1,2,0:T(8,128)(2,1)}, bf16[8,64,1,512]{3,1,2,0:T(8,128)(2,1)S(1)}, u32[]{:S(2)}, u32[]{:S(2)}) collective-permute-start(bf16[8,64,1,512]{3,1,2,0:T(8,128)(2,1)} %get-tuple-element.8), channel_id=1, source_target_pairs={{0,1},{1,2},{2,3},{3,4},{4,5},{5,6},{6,7},{7,8},{8,9},{9,10},{10,1... | collective-permute-start | bytes 1572872 | tf_op jit(solution)/shard_map/ppermute | solution.py:42
  78.9 4.4 %collective-permute-done.1 = bf16[8,64,1,512]{3,1,2,0:T(8,128)(2,1)S(1)} collective-permute-done((bf16[8,64,1,512]{3,1,2,0:T(8,128)(2,1)}, bf16[8,64,1,512]{3,1,2,0:T(8,128)(2,1)S(1)}, u32[]{:S(2)}, u32[]{:S(2)}) %collective-permute-start.1) | collective-permute-done | bytes 524320 | tf_op jit(solution)/shard_map/ppermute | solution.py:43
  83.3 4.9 %collective-permute-done = bf16[8,64,1,512]{3,1,2,0:T(8,128)(2,1)S(1)} collective-permute-done((bf16[8,64,1,512]{3,1,2,0:T(8,128)(2,1)}, bf16[8,64,1,512]{3,1,2,0:T(8,128)(2,1)S(1)}, u32[]{:S(2)}, u32[]{:S(2)}) %collective-permute-start) | collective-permute-done | bytes 524320 | tf_op jit(solution)/shard_map/ppermute | solution.py:42
  89.3 1.4 fusion.48
  90.7 1.4 fusion.52
  92.1 1.4 fusion.51
  93.6 2.5 %fusion.24 = bf16[8,64,2,32]{3,1,2,0:T(8,128)(2,1)S(1)} fusion(f32[8,66,4,288]{3,1,2,0:T(8,128)S(1)} %fusion.48, f32[8,66,4,288]{3,1,2,0:T(8,128)S(1)} %fusion.52, f32[8,66,4,288]{3,1,2,0:T(8,128)S(1)} %fusion.51), kind=kLoop, calls=%fused_computation.36 | loop fusion | flops 884736 | bytes 3604480 | tf_op jit(solution)/shard_map/convert_element_type | solution.py:127
  96.3 2.2 collective-permute-start.2
  98.5 4.1 %collective-permute-start.3 = (bf16[8,4,2,32]{3,0,2,1:T(8,128)(2,1)S(1)}, bf16[8,4,2,32]{3,0,2,1:T(8,128)(2,1)S(1)}, u32[]{:S(2)}, u32[]{:S(2)}) collective-permute-start(bf16[8,4,2,32]{3,0,2,1:T(8,128)(2,1)S(1)} %bitcast.212), channel_id=1, source_target_pairs={{0,64},{32,96},{64,0},{96,32},{128,192},{160,224},{192,128},{224,1... | collective-permute-start | bytes 12296 | tf_op jit(solution)/shard_map/ppermute | solution.py:27
  102.6 4.2 %collective-permute-start.4 = (bf16[8,4,2,32]{3,0,2,1:T(8,128)(2,1)S(1)}, bf16[8,4,2,32]{3,0,2,1:T(8,128)(2,1)S(1)}, u32[]{:S(2)}, u32[]{:S(2)}) collective-permute-start(bf16[8,4,2,32]{3,0,2,1:T(8,128)(2,1)S(1)} %bitcast.211), channel_id=1, source_target_pairs={{0,96},{32,64},{64,32},{96,0},{128,224},{160,192},{192,160},{224,1... | collective-permute-start | bytes 12296 | tf_op jit(solution)/shard_map/ppermute | solution.py:27
  106.8 2.6 %collective-permute-start.5 = (bf16[8,4,2,32]{3,0,2,1:T(8,128)(2,1)S(1)}, bf16[8,4,2,32]{3,0,2,1:T(8,128)(2,1)S(1)}, u32[]{:S(2)}, u32[]{:S(2)}) collective-permute-start(bf16[8,4,2,32]{3,0,2,1:T(8,128)(2,1)S(1)} %bitcast.210), channel_id=1, source_target_pairs={{0,128},{32,160},{64,192},{96,224},{128,0},{160,32},{192,64},{224,... | collective-permute-start | bytes 12296 | tf_op jit(solution)/shard_map/ppermute | solution.py:27
  109.4 1.9 collective-permute-start.6
  111.5 5.6 %collective-permute-start.7 = (bf16[8,4,2,32]{3,0,2,1:T(8,128)(2,1)S(1)}, bf16[8,4,2,32]{3,0,2,1:T(8,128)(2,1)S(1)}, u32[]{:S(2)}, u32[]{:S(2)}) collective-permute-start(bf16[8,4,2,32]{3,0,2,1:T(8,128)(2,1)S(1)} %bitcast.208), channel_id=1, source_target_pairs={{0,192},{32,224},{64,128},{96,160},{128,64},{160,96},{192,0},{224,... | collective-permute-start | bytes 12296 | tf_op jit(solution)/shard_map/ppermute | solution.py:27
  117.1 4.6 %collective-permute-start.8 = (bf16[8,4,2,32]{3,0,2,1:T(8,128)(2,1)S(1)}, bf16[8,4,2,32]{3,0,2,1:T(8,128)(2,1)S(1)}, u32[]{:S(2)}, u32[]{:S(2)}) collective-permute-start(bf16[8,4,2,32]{3,0,2,1:T(8,128)(2,1)S(1)} %bitcast.207), channel_id=1, source_target_pairs={{0,224},{32,192},{64,160},{96,128},{128,96},{160,64},{192,32},{224... | collective-permute-start | bytes 12296 | tf_op jit(solution)/shard_map/ppermute | solution.py:27
  121.7 3.4 %collective-permute-start.9 = (bf16[8,4,2,32]{3,0,2,1:T(8,128)(2,1)S(1)}, bf16[8,4,2,32]{3,0,2,1:T(8,128)(2,1)S(1)}, u32[]{:S(2)}, u32[]{:S(2)}) collective-permute-start(bf16[8,4,2,32]{3,0,2,1:T(8,128)(2,1)S(1)} %bitcast.206), channel_id=1, source_target_pairs={{0,256},{32,288},{64,320},{96,352},{128,384},{160,416},{192,448},{... | collective-permute-start | bytes 12296 | tf_op jit(solution)/shard_map/ppermute | solution.py:27
  125.1 1.9 collective-permute-start.10
  127.1 7.2 %collective-permute-start.11 = (bf16[8,4,2,32]{3,0,2,1:T(8,128)(2,1)S(1)}, bf16[8,4,2,32]{3,0,2,1:T(8,128)(2,1)S(1)}, u32[]{:S(2)}, u32[]{:S(2)}) collective-permute-start(bf16[8,4,2,32]{3,0,2,1:T(8,128)(2,1)S(1)} %bitcast.204), channel_id=1, source_target_pairs={{0,320},{32,352},{64,256},{96,288},{128,448},{160,480},{192,384},{... | collective-permute-start | bytes 12296 | tf_op jit(solution)/shard_map/ppermute | solution.py:27
  134.3 5.2 %collective-permute-start.12 = (bf16[8,4,2,32]{3,0,2,1:T(8,128)(2,1)S(1)}, bf16[8,4,2,32]{3,0,2,1:T(8,128)(2,1)S(1)}, u32[]{:S(2)}, u32[]{:S(2)}) collective-permute-start(bf16[8,4,2,32]{3,0,2,1:T(8,128)(2,1)S(1)} %bitcast.203), channel_id=1, source_target_pairs={{0,352},{32,320},{64,288},{96,256},{128,480},{160,448},{192,416},{... | collective-permute-start | bytes 12296 | tf_op jit(solution)/shard_map/ppermute | solution.py:27
  139.6 2.9 %collective-permute-start.13 = (bf16[8,4,2,32]{3,0,2,1:T(8,128)(2,1)S(1)}, bf16[8,4,2,32]{3,0,2,1:T(8,128)(2,1)S(1)}, u32[]{:S(2)}, u32[]{:S(2)}) collective-permute-start(bf16[8,4,2,32]{3,0,2,1:T(8,128)(2,1)S(1)} %bitcast.202), channel_id=1, source_target_pairs={{0,384},{32,416},{64,448},{96,480},{128,256},{160,288},{192,320},{... | collective-permute-start | bytes 12296 | tf_op jit(solution)/shard_map/ppermute | solution.py:27
  142.5 1.9 collective-permute-start.14
  144.4 7.7 %collective-permute-start.15 = (bf16[8,4,2,32]{3,0,2,1:T(8,128)(2,1)S(1)}, bf16[8,4,2,32]{3,0,2,1:T(8,128)(2,1)S(1)}, u32[]{:S(2)}, u32[]{:S(2)}) collective-permute-start(bf16[8,4,2,32]{3,0,2,1:T(8,128)(2,1)S(1)} %bitcast.200), channel_id=1, source_target_pairs={{0,448},{32,480},{64,384},{96,416},{128,320},{160,352},{192,256},{... | collective-permute-start | bytes 12296 | tf_op jit(solution)/shard_map/ppermute | solution.py:27
  152.2 4.6 %collective-permute-start.16 = (bf16[8,4,2,32]{3,0,2,1:T(8,128)(2,1)S(1)}, bf16[8,4,2,32]{3,0,2,1:T(8,128)(2,1)S(1)}, u32[]{:S(2)}, u32[]{:S(2)}) collective-permute-start(bf16[8,4,2,32]{3,0,2,1:T(8,128)(2,1)S(1)} %bitcast.199), channel_id=1, source_target_pairs={{0,480},{32,448},{64,416},{96,384},{128,352},{160,320},{192,288},{... | collective-permute-start | bytes 12296 | tf_op jit(solution)/shard_map/ppermute | solution.py:27
  156.9 4.3 %collective-permute-done.16 = bf16[8,4,2,32]{3,0,2,1:T(8,128)(2,1)S(1)} collective-permute-done((bf16[8,4,2,32]{3,0,2,1:T(8,128)(2,1)S(1)}, bf16[8,4,2,32]{3,0,2,1:T(8,128)(2,1)S(1)}, u32[]{:S(2)}, u32[]{:S(2)}) %collective-permute-start.16) | collective-permute-done | bytes 4128 | tf_op jit(solution)/shard_map/ppermute | solution.py:27
  163.0 1.9 collective-permute-start.17
  165.0 6.0 %collective-permute-start.18 = (bf16[8,1,4,256]{3,2,1,0:T(4,128)(2,1)S(1)}, bf16[8,1,4,256]{3,2,1,0:T(4,128)(2,1)S(1)}, u32[]{:S(2)}, u32[]{:S(2)}) collective-permute-start(bf16[8,1,4,256]{3,2,1,0:T(4,128)(2,1)S(1)} %get-tuple-element.38), channel_id=1, source_target_pairs={{32,0},{64,32},{96,64},{128,96},{160,128},{192,160},{224,192},{256... | collective-permute-start | bytes 49160 | tf_op jit(solution)/shard_map/ppermute | solution.py:43
  171.1 1.3 collective-permute-done.18
  172.6 1.9 collective-permute-start.20
  174.5 2.6 %collective-permute-start.19 = (bf16[8,10,1,256]{3,2,1,0:T(2,128)(2,1)S(1)}, bf16[8,10,1,256]{3,2,1,0:T(2,128)(2,1)S(1)}, u32[]{:S(2)}, u32[]{:S(2)}) collective-permute-start(bf16[8,10,1,256]{3,2,1,0:T(2,128)(2,1)S(1)} %get-tuple-element.36), channel_id=1, source_target_pairs={{0,1},{1,2},{2,3},{3,4},{4,5},{5,6},{6,7},{7,8},{8,9},{9,10},{10,1... | collective-permute-start | bytes 122888 | tf_op jit(solution)/shard_map/ppermute | solution.py:42
  177.5 3.9 %collective-permute-done.19 = bf16[8,10,1,256]{3,2,1,0:T(2,128)(2,1)S(1)} collective-permute-done((bf16[8,10,1,256]{3,2,1,0:T(2,128)(2,1)S(1)}, bf16[8,10,1,256]{3,2,1,0:T(2,128)(2,1)S(1)}, u32[]{:S(2)}, u32[]{:S(2)}) %collective-permute-start.19) | collective-permute-done | bytes 40992 | tf_op jit(solution)/shard_map/ppermute | solution.py:42
  188.8 3.3 %fusion.41 = (bf16[1,3,3,256,256]{3,4,2,1,0:T(8,128)(2,1)S(1)}, bf16[1,3,3,256,256]{3,4,2,1,0:T(8,128)(2,1)S(1)}, bf16[1,3,3,256,256]{3,4,2,1,0:T(8,128)(2,1)}) fusion(bf16[3,3,3,256,256]{3,4,2,1,0:T(8,128)(2,1)} %all-gather.5.cloned.1.call-done), kind=kLoop, calls=%fused_computation.161 | loop fusion | bytes 7077888 | tf_op jit(solution)/shard_map/slice | solution.py:83
  192.1 2.4 copy.107
  194.5 1.5 copy.108
  196.8 2.4 %fusion.49 = f32[8,8,4,256]{3,2,1,0:T(4,128)S(1)} fusion(bf16[10,8,4,2304]{3,2,1,0:T(4,128)(2,1)} %slice_dynamic-update-slice_fusion.9, bf16[2304,256,1,1]{1,0,3,2:T(8,128)(2,1)} %bitcast.187), kind=kOutput, calls=%fused_computation.169 | convolution fusion | flops 301989888 | bytes 2916352 | tf_op jit(solution)/shard_map/dot_general | solution.py:79
  199.2 2.0 convolution_add_fusion.3
  201.2 2.1 fusion.14
  204.0 6.3 %collective-permute-start.22 = (bf16[8,1,8,128]{3,2,1,0:T(8,128)(2,1)S(1)}, bf16[8,1,8,128]{3,2,1,0:T(8,128)(2,1)S(1)}, u32[]{:S(2)}, u32[]{:S(2)}) collective-permute-start(bf16[8,1,8,128]{3,2,1,0:T(8,128)(2,1)S(1)} %get-tuple-element.19), channel_id=1, source_target_pairs={{32,0},{64,32},{96,64},{128,96},{160,128},{192,160},{224,192},{256... | collective-permute-start | bytes 49160 | tf_op jit(solution)/shard_map/ppermute | solution.py:43
  210.3 1.9 collective-permute-start.21
  212.3 5.8 %collective-permute-done.21 = bf16[8,1,8,128]{3,2,1,0:T(8,128)(2,1)S(1)} collective-permute-done((bf16[8,1,8,128]{3,2,1,0:T(8,128)(2,1)S(1)}, bf16[8,1,8,128]{3,2,1,0:T(8,128)(2,1)S(1)}, u32[]{:S(2)}, u32[]{:S(2)}) %collective-permute-start.21) | collective-permute-done | bytes 16416 | tf_op jit(solution)/shard_map/ppermute | solution.py:42
  218.2 1.9 collective-permute-start.24
  220.1 2.4 %collective-permute-start.23 = (bf16[8,18,1,128]{3,2,1,0:T(2,128)(2,1)S(1)}, bf16[8,18,1,128]{3,2,1,0:T(2,128)(2,1)S(1)}, u32[]{:S(2)}, u32[]{:S(2)}) collective-permute-start(bf16[8,18,1,128]{3,2,1,0:T(2,128)(2,1)S(1)} %get-tuple-element.16), channel_id=1, source_target_pairs={{0,1},{1,2},{2,3},{3,4},{4,5},{5,6},{6,7},{7,8},{8,9},{9,10},{10,1... | collective-permute-start | bytes 110600 | tf_op jit(solution)/shard_map/ppermute | solution.py:42
  222.7 4.3 %collective-permute-done.23 = bf16[8,18,1,128]{3,2,1,0:T(2,128)(2,1)S(1)} collective-permute-done((bf16[8,18,1,128]{3,2,1,0:T(2,128)(2,1)S(1)}, bf16[8,18,1,128]{3,2,1,0:T(2,128)(2,1)S(1)}, u32[]{:S(2)}, u32[]{:S(2)}) %collective-permute-start.23) | collective-permute-done | bytes 36896 | tf_op jit(solution)/shard_map/ppermute | solution.py:42
  230.5 1.5 fusion.12
  (127 shorter events, 16.4 us)
Async XLA Ops:
  7.4 155.0 %copy-start = (bf16[512,256]{1,0:T(8,128)(2,1)S(1)}, bf16[512,256]{1,0:T(8,128)(2,1)}, u32[]{:S(2)}) copy-start(bf16[512,256]{1,0:T(8,128)(2,1)} %param.10) | copy-start | bytes 786436
  7.4 71.5 %copy-start.2 = (bf16[3,3,3,512,32]{3,4,2,1,0:T(8,128)(2,1)S(1)}, bf16[3,3,3,512,32]{3,4,2,1,0:T(8,128)(2,1)}, u32[]{:S(2)}) copy-start(bf16[3,3,3,512,32]{3,4,2,1,0:T(8,128)(2,1)} %param.7) | copy-start | bytes 2654212
  7.4 64.1 %all-gather.3.cloned.1.call-start = ((), (), s32[]{:S(2)}) async-start(), calls=%async_computation | async-start | bytes 1114112 | tf_op jit(solution)/shard_map/all_gather | solution.py:124
  10.0 178.8 %all-gather.5.cloned.1.call-start = ((), (), s32[]{:S(2)}) async-start(), calls=%async_computation.1 | async-start | bytes 3649536 | tf_op jit(solution)/shard_map/all_gather | solution.py:119
  74.4 8.9 %collective-permute-start.1 = (bf16[8,64,1,512]{3,1,2,0:T(8,128)(2,1)}, bf16[8,64,1,512]{3,1,2,0:T(8,128)(2,1)S(1)}, u32[]{:S(2)}, u32[]{:S(2)}) collective-permute-start(bf16[8,64,1,512]{3,1,2,0:T(8,128)(2,1)} %get-tuple-element.9), channel_id=1, source_target_pairs={{1,0},{2,1},{3,2},{4,3},{5,4},{6,5},{7,6},{8,7},{9,8},{10,9},{11,1... | collective-permute-start | bytes 1572872 | tf_op jit(solution)/shard_map/ppermute | solution.py:43
  76.3 11.9 %collective-permute-start = (bf16[8,64,1,512]{3,1,2,0:T(8,128)(2,1)}, bf16[8,64,1,512]{3,1,2,0:T(8,128)(2,1)S(1)}, u32[]{:S(2)}, u32[]{:S(2)}) collective-permute-start(bf16[8,64,1,512]{3,1,2,0:T(8,128)(2,1)} %get-tuple-element.8), channel_id=1, source_target_pairs={{0,1},{1,2},{2,3},{3,4},{4,5},{5,6},{6,7},{7,8},{8,9},{9,10},{10,1... | collective-permute-start | bytes 1572872 | tf_op jit(solution)/shard_map/ppermute | solution.py:42
  96.1 66.3 %copy-start.4 = (bf16[8,4,2,512]{3,2,1,0:T(2,128)(2,1)S(1)}, bf16[8,4,2,512]{3,2,1,0:T(2,128)(2,1)}, u32[]{:S(2)}) copy-start(bf16[8,4,2,512]{3,2,1,0:T(2,128)(2,1)} %param.6) | copy-start | bytes 196612
  96.3 15.2 %collective-permute-start.2 = (bf16[8,4,2,32]{3,0,2,1:T(8,128)(2,1)S(1)}, bf16[8,4,2,32]{3,0,2,1:T(8,128)(2,1)S(1)}, u32[]{:S(2)}, u32[]{:S(2)}) collective-permute-start(bf16[8,4,2,32]{3,0,2,1:T(8,128)(2,1)S(1)} %bitcast.213), channel_id=1, source_target_pairs={{0,32},{32,0},{64,96},{96,64},{128,160},{160,128},{192,224},{224,1... | collective-permute-start | bytes 12296 | tf_op jit(solution)/shard_map/ppermute | solution.py:27
  98.5 18.6 %collective-permute-start.3 = (bf16[8,4,2,32]{3,0,2,1:T(8,128)(2,1)S(1)}, bf16[8,4,2,32]{3,0,2,1:T(8,128)(2,1)S(1)}, u32[]{:S(2)}, u32[]{:S(2)}) collective-permute-start(bf16[8,4,2,32]{3,0,2,1:T(8,128)(2,1)S(1)} %bitcast.212), channel_id=1, source_target_pairs={{0,64},{32,96},{64,0},{96,32},{128,192},{160,224},{192,128},{224,1... | collective-permute-start | bytes 12296 | tf_op jit(solution)/shard_map/ppermute | solution.py:27
  102.6 19.1 %collective-permute-start.4 = (bf16[8,4,2,32]{3,0,2,1:T(8,128)(2,1)S(1)}, bf16[8,4,2,32]{3,0,2,1:T(8,128)(2,1)S(1)}, u32[]{:S(2)}, u32[]{:S(2)}) collective-permute-start(bf16[8,4,2,32]{3,0,2,1:T(8,128)(2,1)S(1)} %bitcast.211), channel_id=1, source_target_pairs={{0,96},{32,64},{64,32},{96,0},{128,224},{160,192},{192,160},{224,1... | collective-permute-start | bytes 12296 | tf_op jit(solution)/shard_map/ppermute | solution.py:27
  106.8 18.3 %collective-permute-start.5 = (bf16[8,4,2,32]{3,0,2,1:T(8,128)(2,1)S(1)}, bf16[8,4,2,32]{3,0,2,1:T(8,128)(2,1)S(1)}, u32[]{:S(2)}, u32[]{:S(2)}) collective-permute-start(bf16[8,4,2,32]{3,0,2,1:T(8,128)(2,1)S(1)} %bitcast.210), channel_id=1, source_target_pairs={{0,128},{32,160},{64,192},{96,224},{128,0},{160,32},{192,64},{224,... | collective-permute-start | bytes 12296 | tf_op jit(solution)/shard_map/ppermute | solution.py:27
  109.4 17.6 %collective-permute-start.6 = (bf16[8,4,2,32]{3,0,2,1:T(8,128)(2,1)S(1)}, bf16[8,4,2,32]{3,0,2,1:T(8,128)(2,1)S(1)}, u32[]{:S(2)}, u32[]{:S(2)}) collective-permute-start(bf16[8,4,2,32]{3,0,2,1:T(8,128)(2,1)S(1)} %bitcast.209), channel_id=1, source_target_pairs={{0,160},{32,128},{64,224},{96,192},{128,32},{160,0},{192,96},{224,... | collective-permute-start | bytes 12296 | tf_op jit(solution)/shard_map/ppermute | solution.py:27
  111.5 22.8 %collective-permute-start.7 = (bf16[8,4,2,32]{3,0,2,1:T(8,128)(2,1)S(1)}, bf16[8,4,2,32]{3,0,2,1:T(8,128)(2,1)S(1)}, u32[]{:S(2)}, u32[]{:S(2)}) collective-permute-start(bf16[8,4,2,32]{3,0,2,1:T(8,128)(2,1)S(1)} %bitcast.208), channel_id=1, source_target_pairs={{0,192},{32,224},{64,128},{96,160},{128,64},{160,96},{192,0},{224,... | collective-permute-start | bytes 12296 | tf_op jit(solution)/shard_map/ppermute | solution.py:27
  117.1 22.4 %collective-permute-start.8 = (bf16[8,4,2,32]{3,0,2,1:T(8,128)(2,1)S(1)}, bf16[8,4,2,32]{3,0,2,1:T(8,128)(2,1)S(1)}, u32[]{:S(2)}, u32[]{:S(2)}) collective-permute-start(bf16[8,4,2,32]{3,0,2,1:T(8,128)(2,1)S(1)} %bitcast.207), channel_id=1, source_target_pairs={{0,224},{32,192},{64,160},{96,128},{128,96},{160,64},{192,32},{224... | collective-permute-start | bytes 12296 | tf_op jit(solution)/shard_map/ppermute | solution.py:27
  121.7 20.8 %collective-permute-start.9 = (bf16[8,4,2,32]{3,0,2,1:T(8,128)(2,1)S(1)}, bf16[8,4,2,32]{3,0,2,1:T(8,128)(2,1)S(1)}, u32[]{:S(2)}, u32[]{:S(2)}) collective-permute-start(bf16[8,4,2,32]{3,0,2,1:T(8,128)(2,1)S(1)} %bitcast.206), channel_id=1, source_target_pairs={{0,256},{32,288},{64,320},{96,352},{128,384},{160,416},{192,448},{... | collective-permute-start | bytes 12296 | tf_op jit(solution)/shard_map/ppermute | solution.py:27
  125.1 19.3 %collective-permute-start.10 = (bf16[8,4,2,32]{3,0,2,1:T(8,128)(2,1)S(1)}, bf16[8,4,2,32]{3,0,2,1:T(8,128)(2,1)S(1)}, u32[]{:S(2)}, u32[]{:S(2)}) collective-permute-start(bf16[8,4,2,32]{3,0,2,1:T(8,128)(2,1)S(1)} %bitcast.205), channel_id=1, source_target_pairs={{0,288},{32,256},{64,352},{96,320},{128,416},{160,384},{192,480},{... | collective-permute-start | bytes 12296 | tf_op jit(solution)/shard_map/ppermute | solution.py:27
  127.1 25.1 %collective-permute-start.11 = (bf16[8,4,2,32]{3,0,2,1:T(8,128)(2,1)S(1)}, bf16[8,4,2,32]{3,0,2,1:T(8,128)(2,1)S(1)}, u32[]{:S(2)}, u32[]{:S(2)}) collective-permute-start(bf16[8,4,2,32]{3,0,2,1:T(8,128)(2,1)S(1)} %bitcast.204), channel_id=1, source_target_pairs={{0,320},{32,352},{64,256},{96,288},{128,448},{160,480},{192,384},{... | collective-permute-start | bytes 12296 | tf_op jit(solution)/shard_map/ppermute | solution.py:27
  134.3 22.5 %collective-permute-start.12 = (bf16[8,4,2,32]{3,0,2,1:T(8,128)(2,1)S(1)}, bf16[8,4,2,32]{3,0,2,1:T(8,128)(2,1)S(1)}, u32[]{:S(2)}, u32[]{:S(2)}) collective-permute-start(bf16[8,4,2,32]{3,0,2,1:T(8,128)(2,1)S(1)} %bitcast.203), channel_id=1, source_target_pairs={{0,352},{32,320},{64,288},{96,256},{128,480},{160,448},{192,416},{... | collective-permute-start | bytes 12296 | tf_op jit(solution)/shard_map/ppermute | solution.py:27
  139.6 17.3 %collective-permute-start.13 = (bf16[8,4,2,32]{3,0,2,1:T(8,128)(2,1)S(1)}, bf16[8,4,2,32]{3,0,2,1:T(8,128)(2,1)S(1)}, u32[]{:S(2)}, u32[]{:S(2)}) collective-permute-start(bf16[8,4,2,32]{3,0,2,1:T(8,128)(2,1)S(1)} %bitcast.202), channel_id=1, source_target_pairs={{0,384},{32,416},{64,448},{96,480},{128,256},{160,288},{192,320},{... | collective-permute-start | bytes 12296 | tf_op jit(solution)/shard_map/ppermute | solution.py:27
  142.5 14.3 %collective-permute-start.14 = (bf16[8,4,2,32]{3,0,2,1:T(8,128)(2,1)S(1)}, bf16[8,4,2,32]{3,0,2,1:T(8,128)(2,1)S(1)}, u32[]{:S(2)}, u32[]{:S(2)}) collective-permute-start(bf16[8,4,2,32]{3,0,2,1:T(8,128)(2,1)S(1)} %bitcast.201), channel_id=1, source_target_pairs={{0,416},{32,384},{64,480},{96,448},{128,288},{160,256},{192,352},{... | collective-permute-start | bytes 12296 | tf_op jit(solution)/shard_map/ppermute | solution.py:27
  144.4 12.4 %collective-permute-start.15 = (bf16[8,4,2,32]{3,0,2,1:T(8,128)(2,1)S(1)}, bf16[8,4,2,32]{3,0,2,1:T(8,128)(2,1)S(1)}, u32[]{:S(2)}, u32[]{:S(2)}) collective-permute-start(bf16[8,4,2,32]{3,0,2,1:T(8,128)(2,1)S(1)} %bitcast.200), channel_id=1, source_target_pairs={{0,448},{32,480},{64,384},{96,416},{128,320},{160,352},{192,256},{... | collective-permute-start | bytes 12296 | tf_op jit(solution)/shard_map/ppermute | solution.py:27
  152.2 9.0 %collective-permute-start.16 = (bf16[8,4,2,32]{3,0,2,1:T(8,128)(2,1)S(1)}, bf16[8,4,2,32]{3,0,2,1:T(8,128)(2,1)S(1)}, u32[]{:S(2)}, u32[]{:S(2)}) collective-permute-start(bf16[8,4,2,32]{3,0,2,1:T(8,128)(2,1)S(1)} %bitcast.199), channel_id=1, source_target_pairs={{0,480},{32,448},{64,416},{96,384},{128,352},{160,320},{192,288},{... | collective-permute-start | bytes 12296 | tf_op jit(solution)/shard_map/ppermute | solution.py:27
  163.0 8.0 %collective-permute-start.17 = (bf16[8,1,4,256]{3,2,1,0:T(4,128)(2,1)S(1)}, bf16[8,1,4,256]{3,2,1,0:T(4,128)(2,1)S(1)}, u32[]{:S(2)}, u32[]{:S(2)}) collective-permute-start(bf16[8,1,4,256]{3,2,1,0:T(4,128)(2,1)S(1)} %get-tuple-element.39), channel_id=1, source_target_pairs={{0,32},{32,64},{64,96},{96,128},{128,160},{160,192},{192,224},{224... | collective-permute-start | bytes 49160 | tf_op jit(solution)/shard_map/ppermute | solution.py:42
  165.0 7.5 %collective-permute-start.18 = (bf16[8,1,4,256]{3,2,1,0:T(4,128)(2,1)S(1)}, bf16[8,1,4,256]{3,2,1,0:T(4,128)(2,1)S(1)}, u32[]{:S(2)}, u32[]{:S(2)}) collective-permute-start(bf16[8,1,4,256]{3,2,1,0:T(4,128)(2,1)S(1)} %get-tuple-element.38), channel_id=1, source_target_pairs={{32,0},{64,32},{96,64},{128,96},{160,128},{192,160},{224,192},{256... | collective-permute-start | bytes 49160 | tf_op jit(solution)/shard_map/ppermute | solution.py:43
  172.6 4.9 %collective-permute-start.20 = (bf16[8,10,1,256]{3,2,1,0:T(2,128)(2,1)S(1)}, bf16[8,10,1,256]{3,2,1,0:T(2,128)(2,1)S(1)}, u32[]{:S(2)}, u32[]{:S(2)}) collective-permute-start(bf16[8,10,1,256]{3,2,1,0:T(2,128)(2,1)S(1)} %get-tuple-element.37), channel_id=1, source_target_pairs={{1,0},{2,1},{3,2},{4,3},{5,4},{6,5},{7,6},{8,7},{9,8},{10,9},{11,1... | collective-permute-start | bytes 122888 | tf_op jit(solution)/shard_map/ppermute | solution.py:43
  174.5 7.0 %collective-permute-start.19 = (bf16[8,10,1,256]{3,2,1,0:T(2,128)(2,1)S(1)}, bf16[8,10,1,256]{3,2,1,0:T(2,128)(2,1)S(1)}, u32[]{:S(2)}, u32[]{:S(2)}) collective-permute-start(bf16[8,10,1,256]{3,2,1,0:T(2,128)(2,1)S(1)} %get-tuple-element.36), channel_id=1, source_target_pairs={{0,1},{1,2},{2,3},{3,4},{4,5},{5,6},{6,7},{7,8},{8,9},{9,10},{10,1... | collective-permute-start | bytes 122888 | tf_op jit(solution)/shard_map/ppermute | solution.py:42
  196.8 2.4 %copy-start.1 = (bf16[1,3,3,256,256]{4,3,2,1,0:T(8,128)(2,1)S(1)}, bf16[1,3,3,256,256]{4,3,2,1,0:T(8,128)(2,1)}, u32[]{:S(2)}) copy-start(bf16[1,3,3,256,256]{4,3,2,1,0:T(8,128)(2,1)} %copy.108) | copy-start | bytes 3538948
  201.2 2.1 copy-start.5
  201.2 21.3 %copy-start.3 = (bf16[3,3,3,128,128]{4,3,2,1,0:T(8,128)(2,1)S(1)}, bf16[3,3,3,128,128]{4,3,2,1,0:T(8,128)(2,1)}, u32[]{:S(2)}) copy-start(bf16[3,3,3,128,128]{4,3,2,1,0:T(8,128)(2,1)} %param.9) | copy-start | bytes 2654212
  204.0 8.3 %collective-permute-start.22 = (bf16[8,1,8,128]{3,2,1,0:T(8,128)(2,1)S(1)}, bf16[8,1,8,128]{3,2,1,0:T(8,128)(2,1)S(1)}, u32[]{:S(2)}, u32[]{:S(2)}) collective-permute-start(bf16[8,1,8,128]{3,2,1,0:T(8,128)(2,1)S(1)} %get-tuple-element.19), channel_id=1, source_target_pairs={{32,0},{64,32},{96,64},{128,96},{160,128},{192,160},{224,192},{256... | collective-permute-start | bytes 49160 | tf_op jit(solution)/shard_map/ppermute | solution.py:43
  210.3 7.7 %collective-permute-start.21 = (bf16[8,1,8,128]{3,2,1,0:T(8,128)(2,1)S(1)}, bf16[8,1,8,128]{3,2,1,0:T(8,128)(2,1)S(1)}, u32[]{:S(2)}, u32[]{:S(2)}) collective-permute-start(bf16[8,1,8,128]{3,2,1,0:T(8,128)(2,1)S(1)} %get-tuple-element.18), channel_id=1, source_target_pairs={{0,32},{32,64},{64,96},{96,128},{128,160},{160,192},{192,224},{224... | collective-permute-start | bytes 49160 | tf_op jit(solution)/shard_map/ppermute | solution.py:42
  218.2 4.5 %collective-permute-start.24 = (bf16[8,18,1,128]{3,2,1,0:T(2,128)(2,1)S(1)}, bf16[8,18,1,128]{3,2,1,0:T(2,128)(2,1)S(1)}, u32[]{:S(2)}, u32[]{:S(2)}) collective-permute-start(bf16[8,18,1,128]{3,2,1,0:T(2,128)(2,1)S(1)} %get-tuple-element.17), channel_id=1, source_target_pairs={{1,0},{2,1},{3,2},{4,3},{5,4},{6,5},{7,6},{8,7},{9,8},{10,9},{11,1... | collective-permute-start | bytes 110600 | tf_op jit(solution)/shard_map/ppermute | solution.py:43
  220.1 6.9 %collective-permute-start.23 = (bf16[8,18,1,128]{3,2,1,0:T(2,128)(2,1)S(1)}, bf16[8,18,1,128]{3,2,1,0:T(2,128)(2,1)S(1)}, u32[]{:S(2)}, u32[]{:S(2)}) collective-permute-start(bf16[8,18,1,128]{3,2,1,0:T(2,128)(2,1)S(1)} %get-tuple-element.16), channel_id=1, source_target_pairs={{0,1},{1,2},{2,3},{3,4},{4,5},{5,6},{6,7},{7,8},{8,9},{9,10},{10,1... | collective-permute-start | bytes 110600 | tf_op jit(solution)/shard_map/ppermute | solution.py:42
Sparse Core Ops, SparseCore 0:
  11.2 60.2 all-gather.2
Sparse Core Ops, SparseCore 1:
  78.8 75.0 all-gather.4
